TPU v7x, 128 devices: a whole 4x4x4 slice. The times are simulated.
128 devices in a mesh: grp: 8 (over z, core), sub: 16 (over y, x).
Axes of the slice: x: 4, y: 4, z: 4, core: 2. Of those that a mesh axis runs over, the one named last changes fastest.
Arguments:
- features: bfloat16 [512, 8, 8, 512], P(('grp', 'sub')), may hold values from -6 to 6
- conv_weight: bfloat16 [27, 64, 64], replicated, may hold values from -0.15625 to 0.15625
- down_weight: bfloat16 [64, 128], replicated, may hold values from -0.75 to 0.75
- cotangent: bfloat16 [128, 512, 128], P(('grp', 'sub')), may hold values from -24 to 24
- src_table: int32 [512, 26], P(('grp', 'sub')), may hold values from -1 to 535
- send_list: int32 [128, 128, 4], P(('grp', 'sub')), may hold values from -1 to 23, as said below
- child_map: int32 [512], P(('grp', 'sub')), may hold values from -1 to 1023, as said below
Outputs:
- coarse: bfloat16 [128, 512, 128], P(('grp', 'sub'))
- grad_input: bfloat16 [512, 8, 8, 512], P(('grp', 'sub'))
- grad_conv: float32 [27, 64, 64], replicated
- grad_down: float32 [64, 128], replicated
Inputs may be any that keep to these rules, and one draw needn't show every extreme that they name: `send_list`: entry [p, r, k] is -1 or 6 times a live slot of device p plus a face number; the used slots of [p, r] come first; device p sends faces only to devices within 16 of p in cyclic device order or exactly 64 away, at most 4 to one device, and some pair sends exactly 4 in every draw. `child_map`: -1 exactly on slots that are not live; live bricks of one super-range have distinct values.
All inputs are finite; a program needn't handle non-finite values.
Results may differ from a plain program's by a relative error of at most 0.0058.
Values may be sent and summed in bfloat16 or wider, within the bound.
A program may use at most 128 MiB of HBM per device.

v0:
```python
import jax
import jax.numpy as jnp
from jax import lax
from jax.experimental import pallas as pl
from jax.experimental.pallas import tpu as pltpu
from jax.sharding import PartitionSpec as P

MESH = pl.DeviceIdType.MESH
N_GRP, N_SUB = 8, 16
PEERS = N_GRP * N_SUB
NEAR = 33
C = 64
F32, BF16 = jnp.float32, jnp.bfloat16
LOCAL = 24
DUMP = LOCAL + 4 * NEAR
TABLE = DUMP + 4
VMEM_LIMIT = 58 * 1024 * 1024
TERMS = 4 * 26
SLOTS = 4 * NEAR

OFFSETS = [
    (x, y, z)
    for x in (-1, 0, 1)
    for y in (-1, 0, 1)
    for z in (-1, 0, 1)
    if (x, y, z) != (0, 0, 0)
]
NUMBER = {offset: number for number, offset in enumerate(OFFSETS)}


def step_of(j):
    return jnp.where(j < 16, j + 1, jnp.where(j == 16, 64, j + 95))


def twin(j):
    return NEAR - 1 - j


def near_of(step):
    return jnp.where(step <= 16, step - 1, jnp.where(step == 64, 16, step - 95))


def coords(device):
    return (device // N_SUB, device % N_SUB)


def lane_iota(rows):
    return lax.broadcasted_iota(jnp.int32, (rows, 128), 1)


def row_iota(rows):
    return lax.broadcasted_iota(jnp.int32, (rows, 128), 0)


def half(tile):
    return pltpu.roll(tile, 64, axis=1)


def lows(rows):
    return lane_iota(rows) < 64


def to_face(tiles):
    top = jnp.concatenate([tiles[0], tiles[1]], axis=1)
    bottom = jnp.concatenate([tiles[2], tiles[3]], axis=1)
    return jnp.concatenate([top, bottom], axis=0)


def from_face(face):
    face = face.astype(F32)
    return [face[0:8, 0:128], face[0:8, 128:256], face[8:16, 0:128], face[8:16, 128:256]]


def widen(tiles, below, above):
    low = lows(tiles[0].shape[0])
    rolled = [half(tile) for tile in tiles]
    result = [jnp.where(low, half(below), rolled[0])]
    for m in range(1, 4):
        result.append(jnp.where(low, rolled[m - 1], rolled[m]))
    result.append(jnp.where(low, rolled[3], half(above)))
    return result


def narrow(tiles):
    low = lows(tiles[0].shape[0])
    rolled = [half(tile) for tile in tiles]
    return [jnp.where(low, rolled[q], rolled[q + 1]) for q in range(4)]


def roll8(value, shift):
    rows = value.shape[0]
    grouped = value.reshape(rows // 8, 8, 128)
    return pltpu.roll(grouped, shift % 8, axis=1).reshape(rows, 128)

def loop(count, body, start=0):
    def step(i, _):
        body(i)
        return 0

    lax.fori_loop(start, count, step, 0)


def column_max(value):
    best = value[0:8]
    for i in range(1, 16):
        best = jnp.maximum(best, value[8 * i : 8 * i + 8])
    for shift in (4, 2, 1):
        best = jnp.maximum(best, pltpu.roll(best, shift, axis=0))
    return best


def index_tables(src_v, send_v, ids, me):
    whole = (128, 128)
    below = lax.broadcasted_iota(jnp.int32, whole, 0)
    along = lax.broadcasted_iota(jnp.int32, whole, 1)
    rows = [jnp.broadcast_to(src_v[b : b + 1, :], whole) for b in range(4)]
    columns = [row.T for row in rows]

    def pick(cases, none):
        best = None
        for match, value in cases:
            value = jnp.where(match, value, -1)
            best = value if best is None else jnp.maximum(best, value)
        best = column_max(best)
        return jnp.where(best < 0, none, best)[0:1]

    for b in range(4):
        cases = []
        for c in range(b + 1):
            match = jnp.logical_and(columns[c] == rows[b], columns[c] >= 0)
            if c == b:
                match = jnp.logical_and(match, below < along)
            cases.append((match, 26 * c + below))
        ids[b : b + 1, :] = pick(cases, TERMS)
    for k in range(4):
        code = jnp.where(along < NEAR, LOCAL + 4 * ((me + step_of(along)) & (PEERS - 1)) + k, -5)
        ids[4 + k : 5 + k, :] = pick([(columns[b] == code, 26 * b + below) for b in range(4)], TERMS)
    code = jnp.where(along < LOCAL, along, -5)
    ids[8:9, :] = pick([(columns[b] == code, 26 * b + below) for b in range(4)], TERMS)

    def number(device):
        return 4 * jnp.clip(near_of((device - me) & (PEERS - 1)), 0, NEAR - 1)

    columns = [jnp.broadcast_to(send_v[:, k : k + 1], whole) for k in range(4)]
    rows = [column.T for column in columns]
    first, second = number(below), number(along)
    for k in range(4):
        cases = []
        for c in range(4):
            match = jnp.logical_and(columns[c] == rows[k], columns[c] >= 0)
            cases.append((jnp.logical_and(match, first + c < second + k), first + c))
        ids[9 + k : 10 + k, :] = pick(cases, SLOTS)
    ids[13:14, :] = pick([(columns[c] == along, first + c) for c in range(4)], SLOTS)


def block_kernel(
    feat_h, cw_h, dw_h, cot_h, src_h, send_h, child_s,
    coarse_h, grad_h, conv_h, down_h,
    feat, cw, dw, cot, src_s, src_p, src_v, send_s, send_v, ids, ids_s,
    flat, faces, table, sbuf, returned, key_s, key_r, dwp, tg_s, tg_r, place,
    band, bandt, zrim, yrim, pad, pre, pg, pgt, acc_a, term, inner,
    tile_s, tile_r, convt, rs1, tot, rs2, fin, ag1, ag1b, ag2, chain,
    coarse, grad, conv_v, down_v,
    face_ss, face_rs, back_ss, back_rs, key_ss, key_rs, tg_ss, tg_rs, tile_ss, tile_rs,
    one_ss, one_rs, oneb_ss, oneb_rs, two_ss, two_rs, three_ss, three_rs, four_ss, four_rs, in_sem, out_sem,
):
    grp, sub = lax.axis_index("grp"), lax.axis_index("sub")
    me = grp * N_SUB + sub

    barrier = pltpu.get_barrier_semaphore()

    def signal(peer):
        pl.semaphore_signal(barrier, inc=1, device_id=peer, device_id_type=MESH)

    def near_peer(j):
        return coords(lax.rem(me + step_of(j), PEERS))

    loop(NEAR, lambda j: signal(near_peer(j)))
    for far in (2, 3, 5, 6):
        signal((lax.rem(grp + far, N_GRP), sub))

    loads = [
        pltpu.make_async_copy(source, target, in_sem.at[i])
        for i, (source, target) in enumerate(
            (
                (feat_h, feat), (send_h, send_s), (send_h, send_v), (cw_h, cw), (cot_h, cot), (dw_h, dw),
                (src_h, src_s), (src_h, src_p),
            )
        )
    ]
    for load in loads:
        load.start()
    loads[0].wait()

    low8, row8 = lows(8), row_iota(8)
    for b in range(4):
        for x in range(8):
            v = feat[b, x].astype(F32)
            for q in range(4):
                flat[q * 256 + b * 64 + x * 8 : q * 256 + b * 64 + x * 8 + 8, :] = v[:, 128 * q : 128 * q + 128]

    def rows(q, b, y):
        return flat[pl.ds(q * 256 + b * 64 + y, 8, stride=8), :]

    def face(number, tiles):
        value = to_face(tiles).astype(BF16)
        faces[number] = value
        table[number] = value

    for b in range(4):
        for s, x in ((0, 0), (1, 7)):
            v = feat[b, x].astype(F32)
            face(b * 6 + s, [v[:, 128 * q : 128 * q + 128] for q in range(4)])
        for s, y in ((2, 0), (3, 7)):
            face(b * 6 + s, [rows(q, b, y) for q in range(4)])
        first = [rows(0, b, y) for y in range(8)]
        last = [rows(3, b, y) for y in range(8)]
        face(b * 6 + 4, [jnp.where(low8, first[2 * q], half(first[2 * q + 1])) for q in range(4)])
        face(b * 6 + 5, [jnp.where(low8, half(last[2 * q]), last[2 * q + 1]) for q in range(4)])
    table[DUMP] = jnp.zeros((16, 256), BF16)
    for b in range(4):
        key_s[b : b + 1] = jnp.full((1, 128), 8 * child_s[b], jnp.int32)
    loads[1].wait()

    def pack(j):
        peer = lax.rem(me + step_of(j), PEERS)
        for k in range(4):
            sbuf[j, k] = faces[jnp.maximum(send_s[0, peer, k], 0)]

    loop(NEAR, pack)
    key_s[4:8] = jnp.zeros((4, 128), jnp.int32)
    key_r[sub] = key_s[...]
    pl.semaphore_wait(barrier, NEAR + 4)

    def sub_copy(s, src, dst, send_sem, recv_sem, arrival):
        other = lax.rem(sub + s, N_SUB)
        slot = other if arrival else sub
        return pltpu.make_async_remote_copy(
            src_ref=src(other), dst_ref=dst.at[slot], send_sem=send_sem.at[other], recv_sem=recv_sem.at[slot],
            device_id=(grp, other), device_id_type=MESH,
        )

    def grp_copy(s, src, dst, send_sem, recv_sem, arrival):
        other = lax.rem(grp + s, N_GRP)
        slot = other if arrival else grp
        return pltpu.make_async_remote_copy(
            src_ref=src(other), dst_ref=dst(slot), send_sem=send_sem.at[other], recv_sem=recv_sem.at[slot],
            device_id=(other, sub), device_id_type=MESH,
        )

    def near_copy(j, dst, send_sem, recv_sem, arrival):
        slot = j if arrival else twin(j)
        return pltpu.make_async_remote_copy(
            src_ref=sbuf.at[j], dst_ref=dst(slot), send_sem=send_sem.at[j], recv_sem=recv_sem.at[slot],
            device_id=near_peer(j), device_id_type=MESH,
        )

    def key_copy(s, arrival):
        return sub_copy(s, lambda other: key_s, key_r, key_ss, key_rs, arrival)

    def tg_copy(s, arrival):
        return sub_copy(s, lambda other: tg_s.at[other], tg_r, tg_ss, tg_rs, arrival)

    def tile_copy(s, arrival):
        return sub_copy(s, lambda other: tile_s, tile_r, tile_ss, tile_rs, arrival)

    def face_copy(j, arrival):
        return near_copy(j, lambda slot: table.at[pl.ds(LOCAL + 4 * slot, 4)], face_ss, face_rs, arrival)

    def back_copy(j, arrival):
        return near_copy(j, lambda slot: returned.at[slot], back_ss, back_rs, arrival)

    def one_copy(s, arrival):
        return grp_copy(
            s, lambda other: convt.at[other, pl.ds(0, 112)], lambda slot: rs1.at[slot, pl.ds(0, 112)],
            one_ss, one_rs, arrival,
        )

    def oneb_copy(s, arrival):
        return grp_copy(
            s, lambda other: convt.at[other, pl.ds(112, 16)], lambda slot: rs1.at[slot, pl.ds(112, 16)],
            oneb_ss, oneb_rs, arrival,
        )

    def two_copy(s, arrival):
        return sub_copy(s, lambda other: tot.at[pl.ds(8 * other, 8)], rs2, two_ss, two_rs, arrival)

    def three_copy(s, arrival):
        return sub_copy(s, lambda other: fin, ag1, three_ss, three_rs, arrival)

    def four_copy(s, arrival):
        return grp_copy(s, lambda other: ag1b, lambda slot: ag2.at[slot], four_ss, four_rs, arrival)

    loop(N_SUB, lambda s: key_copy(s, False).start(), 1)
    loop(NEAR, lambda j: face_copy(j, False).start())

    for load in loads[2:]:
        load.wait()
    band[...] = jnp.zeros_like(band)
    bandt[...] = jnp.zeros_like(bandt)
    for n in range(9):
        for s in range(3):
            w = cw[3 * n + s]
            band[n, 64 * s : 64 * s + 64, 0:64] = w
            band[n, 64 * s + 64 : 64 * s + 128, 64:128] = w
            d = 2 - s
            bandt[n, 0:64, 64 * d : 64 * d + 64] = w
            bandt[n, 64:128, 64 * d + 64 : 64 * d + 128] = w
    src_v[...] = jnp.full((8, 128), -1, jnp.int32)
    src_v[0:4, 0:26] = src_p[...]
    index_tables(src_v, send_v.at[0], ids, me)
    to_scalars = pltpu.make_async_copy(ids, ids_s, in_sem.at[8])
    to_scalars.start()
    pg[...] = jnp.zeros_like(pg)
    term[TERMS] = jnp.zeros((8, 512), F32)
    chain[SLOTS] = jnp.zeros((8, 512), F32)
    dwp[0:64] = dw[...]
    dwp[64:128] = dw[...]
    coarse_grad = lax.dot_general(
        cot[0], dwp[...], (((1,), (1,)), ((), ())), preferred_element_type=F32
    ).astype(BF16)

    def voxel_key(shape, dim):
        v = lax.broadcasted_iota(jnp.int32, shape, dim)
        x, y, z = v >> 6, (v >> 3) & 7, v & 7
        spot = 16 * (x >> 1) + 4 * (y >> 1) + (z >> 1)
        inside = 4 * (x & 1) + 2 * (y & 1) + (z & 1)
        return (64 * sub + spot) * 8 + inside

    loop(N_SUB, lambda s: key_copy(s, True).wait_recv(), 1)
    ijk = row_iota(8)
    keys = jnp.concatenate(
        [jnp.broadcast_to(key_r[s, b : b + 1, :], (8, 128)) + ijk for s in range(N_SUB) for b in range(4)], axis=0
    )
    wanted = jnp.broadcast_to(voxel_key((1, 512), 1), (512, 512))
    take = jnp.where(jnp.concatenate([keys] * 4, axis=1) == wanted, 1.0, 0.0).astype(BF16)
    tiles = jnp.dot(take, coarse_grad, preferred_element_type=F32).astype(BF16)
    tg_s[...] = tiles.reshape(N_SUB, 32, 128)
    tg_r[sub] = tg_s[sub]
    loop(N_SUB, lambda s: tg_copy(s, False).start(), 1)
    key_row = jnp.concatenate([keys[128 * q : 128 * q + 128].T for q in range(4)], axis=1)[0:1]
    place[...] = jnp.where(
        jnp.broadcast_to(key_row, (512, 512)) == jnp.broadcast_to(voxel_key((512, 1), 0), (512, 512)), 1.0, 0.0
    ).astype(BF16)
    to_scalars.wait()
    loop(NEAR, lambda j: face_copy(j, True).wait_recv())

    def slab(b, offset):
        code = src_s[b, NUMBER[offset]]
        remote = code - LOCAL
        spot = LOCAL + 4 * near_of(((remote >> 2) - me) & (PEERS - 1)) + (remote & 3)
        return from_face(table[jnp.where(code < 0, DUMP, jnp.where(code < LOCAL, code, spot))])

    for b in range(4):
        below, above = slab(b, (0, 0, -1)), slab(b, (0, 0, 1))
        for y in range(8):
            q = y // 2
            if y % 2 == 0:
                value = jnp.where(low8, above[q], half(below[q]))
            else:
                value = jnp.where(low8, half(above[q]), below[q])
            zrim[pl.ds(b * 8 + y, 8, stride=32), :] = value
        for dy, row in ((-1, 7), (1, 0)):
            wide = widen(slab(b, (0, dy, 0)), slab(b, (0, dy, -1))[3], slab(b, (0, dy, 1))[0])
            for m in range(5):
                yrim[pl.ds(m * 256 + b * 8 + row, 8, stride=32), :] = wide[m]

    def put(m, first, value, before, after):
        count = value.shape[0]
        lanes = slice(128 * m, 128 * m + 128)
        row = row_iota(count) & 7
        pad[1, first : first + count, lanes] = value.astype(BF16)
        pad[0, first : first + count, lanes] = roll8(jnp.where(row == 7, before, value), 1).astype(BF16)
        pad[2, first : first + count, lanes] = roll8(jnp.where(row == 0, after, value), -1).astype(BF16)

    for dx, plane in ((-1, 0), (1, 9)):
        parts = [[], [], []]
        for b in range(4):
            for i, dy in enumerate((-1, 0, 1)):
                parts[i].append(
                    widen(slab(b, (dx, dy, 0)), slab(b, (dx, dy, -1))[3], slab(b, (dx, dy, 1))[0])
                )
        for m in range(5):
            before, value, after = [
                jnp.concatenate([part[b][m] for b in range(4)], axis=0) for part in parts
            ]
            put(m, plane * 32, value, before, after)
    for x in range(8):
        inside = []
        for q in range(4):
            inside.append(
                jnp.concatenate([feat[b, x][:, 128 * q : 128 * q + 128].astype(F32) for b in range(4)], axis=0)
            )
        rim = zrim[32 * x : 32 * x + 32, :]
        wide = widen(inside, rim, rim)
        for m in range(5):
            edge = yrim[m * 256 + 32 * x : m * 256 + 32 * x + 32, :]
            put(m, 32 * x + 32, wide[m], edge, edge)

    for m in range(4):
        total = None
        for n in range(9):
            sx, sy = n // 3, n % 3
            product = jnp.dot(
                pad[sy, 32 * sx : 32 * sx + 256, 128 * m : 128 * m + 256], band[n], preferred_element_type=F32
            )
            total = product if total is None else total + product
        pre[256 * m : 256 * m + 256] = total

    loop(N_SUB, lambda s: tg_copy(s, True).wait_recv(), 1)
    grad_tile = tg_r[0].astype(F32)
    for s in range(1, N_SUB):
        grad_tile += tg_r[s].astype(F32)
    grad_tile = grad_tile.reshape(4, 8, 128)
    sub_row = lax.broadcasted_iota(jnp.int32, (4, 8, 128), 1)
    pooled = jnp.zeros((4, 8, 128), F32)
    for top in range(2):
        for deep in range(2):
            spread = jnp.where(
                sub_row < 4,
                jnp.broadcast_to(grad_tile[:, 4 * top + deep : 4 * top + deep + 1, :], (4, 8, 128)),
                jnp.broadcast_to(grad_tile[:, 4 * top + 2 + deep : 4 * top + 3 + deep, :], (4, 8, 128)),
            ).reshape(32, 128) * (1.0 / 64.0)
            total = jnp.zeros((32, 128), F32)
            for m in (2 * deep, 2 * deep + 1):
                for x in range(4 * top, 4 * top + 4):
                    u = pre[256 * m + 32 * x : 256 * m + 32 * x + 32, :]
                    g = 1.0 / (1.0 + jnp.exp(-u))
                    total += u * g
                    slope = g * (1.0 + u * (1.0 - g))
                    pg[64 + 32 * x : 96 + 32 * x, 128 * m + 128 : 128 * m + 256] = (spread * slope).astype(BF16)
            total = total + half(total)
            grouped = total.reshape(4, 8, 128)
            grouped = grouped + pltpu.roll(grouped, 7, axis=1)
            grouped = grouped + pltpu.roll(grouped, 6, axis=1)
            for mid in range(2):
                pooled = jnp.where(
                    sub_row == 4 * top + 2 * mid + deep,
                    jnp.broadcast_to(grouped[:, 4 * mid : 4 * mid + 1, :], (4, 8, 128)),
                    pooled,
                )
    pooled = pooled.reshape(32, 128) * (1.0 / 64.0)
    tile_s[...] = jnp.where(lows(32), pooled, 0.0).astype(BF16)
    tile_r[sub] = tile_s[...]
    loop(N_SUB, lambda s: tile_copy(s, False).start(), 1)

    for m in range(4):
        pgt[:, 256 * m : 256 * m + 256] = (
            pg[64:320, 128 * m + 128 : 128 * m + 256].astype(F32).T.astype(BF16)
        )
    low64 = lows(64)

    def keep(chunk, value):
        for g in range(N_GRP):
            convt[g, 8 * chunk : 8 * chunk + 8] = value[8 * g : 8 * g + 8]

    held = None
    for n in range(9):
        sx, sy = n // 3, n % 3
        total = None
        for m in range(4):
            product = jnp.dot(
                pgt[:, 256 * m : 256 * m + 256],
                pad[sy, 32 * sx : 32 * sx + 256, 128 * m : 128 * m + 256],
                preferred_element_type=F32,
            )
            total = product if total is None else total + product
        r0, r1 = half(total[64:128, 0:128]), half(total[64:128, 128:256])
        first = total[0:64, 0:128] + jnp.where(low64, r0, r1)
        second = total[0:64, 128:256] + r1
        at = 3 * (n // 2)
        if n % 2 == 0:
            keep(at, first)
            held = second
        else:
            turned = half(first)
            keep(at + 1, jnp.where(low64, held, turned))
            keep(at + 2, jnp.where(low64, turned, half(second)))
    keep(13, jnp.where(low64, held, 0.0))
    loop(N_GRP, lambda s: one_copy(s, False).start(), 1)

    for sy in range(3):
        for m in range(5):
            total = None
            for sx in range(3):
                product = lax.dot_general(
                    pg[32 * (2 - sx) : 32 * (2 - sx) + 320, 128 * m : 128 * m + 256],
                    bandt[3 * sx + sy],
                    (((1,), (1,)), ((), ())),
                    preferred_element_type=F32,
                )
                total = product if total is None else total + product
            acc_a[(sy * 5 + m) * 320 : (sy * 5 + m) * 320 + 320, :] = total

    def part(sy, m, first, count):
        return acc_a[(sy * 5 + m) * 320 + first : (sy * 5 + m) * 320 + first + count, :]

    def middle(m, first, count):
        row = row_iota(count) & 7
        return (
            part(1, m, first, count)
            + jnp.where(row < 7, roll8(part(0, m, first, count), -1), 0.0)
            + jnp.where(row > 0, roll8(part(2, m, first, count), 1), 0.0)
        )

    for x in range(8):
        wide = [middle(m, 32 * x + 32, 32) for m in range(5)]
        for q, tile in enumerate(narrow(wide)):
            inner[256 * q + 32 * x : 256 * q + 32 * x + 32, :] = tile
        zrim[32 * x : 32 * x + 32, :] = jnp.where(lows(32), wide[0], wide[4])

    planes = {}
    for dx, plane in ((-1, 0), (1, 9)):
        for b in range(4):
            first = 32 * plane + 8 * b
            planes[dx, 0, b] = [middle(m, first, 8) for m in range(5)]
            planes[dx, -1, b] = [
                jnp.where(row8 == 7, roll8(part(0, m, first, 8), -1), 0.0) for m in range(5)
            ]
            planes[dx, 1, b] = [
                jnp.where(row8 == 0, roll8(part(2, m, first, 8), 1), 0.0) for m in range(5)
            ]

    def rim(b, offset):
        dx, dy, dz = offset
        if dx == 0 and dy == 0:
            rims = [zrim[pl.ds(b * 8 + y, 8, stride=32), :] for y in range(8)]
            if dz < 0:
                return [jnp.where(low8, rims[2 * q], half(rims[2 * q + 1])) for q in range(4)]
            return [jnp.where(low8, half(rims[2 * q]), rims[2 * q + 1]) for q in range(4)]
        if dx != 0:
            wide = planes[dx, dy, b]
        else:
            sy, row = (0, 0) if dy < 0 else (2, 7)
            wide = [
                acc_a[pl.ds((sy * 5 + m) * 320 + 32 + b * 8 + row, 8, stride=32), :] for m in range(5)
            ]
        if dz == 0:
            return narrow(wide)
        if dz > 0:
            return [jnp.where(low8, half(wide[4]), 0.0), None, None, None]
        return [None, None, None, jnp.where(low8, 0.0, half(wide[0]))]

    for b in range(4):
        for t, offset in enumerate(OFFSETS):
            earlier = ids_s[b, t]
            for q, tile in enumerate(rim(b, offset)):
                value = term[earlier, :, 128 * q : 128 * q + 128]
                term[26 * b + t, :, 128 * q : 128 * q + 128] = value if tile is None else value + tile

    def leave(j):
        face_copy(j, False).wait_send()
        for k in range(4):
            value = term[ids_s[4 + k, j]]
            sbuf[j, k] = to_face([value[:, 128 * q : 128 * q + 128] for q in range(4)]).astype(BF16)
        back_copy(j, False).start()

    loop(NEAR, leave)

    loop(N_SUB, lambda s: tile_copy(s, True).wait_recv(), 1)
    coarse_in = jnp.dot(place[...], tile_r[...].reshape(512, 128), preferred_element_type=F32)
    dwp[64:128] = jnp.zeros((64, 128), BF16)
    down = jnp.dot(coarse_in.T.astype(BF16), cot[0], preferred_element_type=F32)
    for g in range(N_GRP):
        convt[g, 112:120] = down[8 * g : 8 * g + 8]
        convt[g, 120:128] = jnp.zeros((8, 128), F32)
    loop(N_GRP, lambda s: oneb_copy(s, False).start(), 1)
    coarse[0] = jnp.dot(coarse_in.astype(BF16), dwp[...], preferred_element_type=F32).astype(BF16)
    coarse_store = pltpu.make_async_copy(coarse, coarse_h, out_sem.at[0])
    coarse_store.start()
    rs1[grp] = convt[grp]

    def both_arrivals(s):
        one_copy(s, True).wait_recv()
        oneb_copy(s, True).wait_recv()

    loop(N_GRP, both_arrivals, 1)
    total = rs1[0]
    for g in range(1, N_GRP):
        total += rs1[g]
    tot[...] = total
    loop(N_SUB, lambda s: two_copy(s, False).start(), 1)
    rs2[sub] = tot[pl.ds(pl.multiple_of(8 * sub, 8), 8), :]
    loop(N_SUB, lambda s: two_copy(s, True).wait_recv(), 1)
    total = rs2[0]
    for s in range(1, N_SUB):
        total += rs2[s]
    fin[...] = total
    loop(N_SUB, lambda s: three_copy(s, False).start(), 1)
    ag1[sub] = fin[...]
    loop(N_SUB, lambda s: three_copy(s, True).wait_recv(), 1)
    ag1b[...] = ag1[...].reshape(128, 128).astype(BF16)
    loop(N_GRP, lambda s: four_copy(s, False).start(), 1)
    ag2[grp] = ag1b[...]

    def take_back(j):
        back_copy(j, True).wait_recv()
        peer = lax.rem(me + step_of(j), PEERS)
        for k in range(4):
            value = chain[ids_s[9 + k, peer]]
            tiles = from_face(returned[j, k])
            for q in range(4):
                chain[4 * j + k, :, 128 * q : 128 * q + 128] = value[:, 128 * q : 128 * q + 128] + tiles[q]

    loop(NEAR, take_back)

    face_sums = [term[ids_s[8, f]] + chain[ids_s[13, f]] for f in range(LOCAL)]

    def tile_of(f, q):
        return face_sums[f][:, 128 * q : 128 * q + 128]

    for b in range(4):
        for f, row in ((2, 0), (3, 7)):
            for q in range(4):
                yrim[pl.ds(q * 256 + b * 8 + row, 8, stride=32), :] = tile_of(6 * b + f, q)
        for y in range(8):
            below, above = tile_of(6 * b + 4, y // 2), tile_of(6 * b + 5, y // 2)
            if y % 2 == 0:
                value = jnp.where(low8, below, half(above))
            else:
                value = jnp.where(low8, half(below), above)
            zrim[pl.ds(b * 8 + y, 8, stride=32), :] = value
    edge = jnp.logical_or(row8 == 0, row8 == 7)
    for b in range(4):
        for x in range(8):
            at = 32 * x + 8 * b
            rim_z = zrim[at : at + 8, :]
            tiles = []
            for q in range(4):
                value = inner[256 * q + at : 256 * q + at + 8, :]
                if x == 0 or x == 7:
                    value = value + tile_of(6 * b + (0 if x == 0 else 1), q)
                value = value + jnp.where(edge, yrim[256 * q + at : 256 * q + at + 8, :], 0.0)
                if q == 0:
                    value = value + jnp.where(low8, rim_z, 0.0)
                if q == 3:
                    value = value + jnp.where(low8, 0.0, rim_z)
                tiles.append(value)
            grad[b, x] = jnp.concatenate(tiles, axis=1).astype(BF16)
    grad_store = pltpu.make_async_copy(grad, grad_h, out_sem.at[1])
    grad_store.start()

    loop(N_GRP, lambda s: four_copy(s, True).wait_recv(), 1)
    got = [ag2[g].astype(F32) for g in range(N_GRP)]
    for s in range(15):
        value = jnp.concatenate([got[g][8 * s : 8 * s + 8] for g in range(N_GRP)], axis=0)
        if s == 14:
            down_v[...] = value
        else:
            turned = value.T
            conv_v[2 * s] = turned[0:64]
            if s < 13:
                conv_v[2 * s + 1] = turned[64:128]
    conv_store = pltpu.make_async_copy(conv_v, conv_h, out_sem.at[2])
    conv_store.start()
    down_store = pltpu.make_async_copy(down_v, down_h, out_sem.at[3])
    down_store.start()

    def sub_ends(s):
        for copy in (key_copy, tg_copy, tile_copy, two_copy, three_copy):
            copy(s, False).wait_send()

    def grp_ends(s):
        for copy in (one_copy, oneb_copy, four_copy):
            copy(s, False).wait_send()

    loop(N_SUB, sub_ends, 1)
    loop(N_GRP, grp_ends, 1)
    loop(NEAR, lambda j: back_copy(j, False).wait_send())
    for store in (coarse_store, grad_store, conv_store, down_store):
        store.wait()


def dma(*shape):
    return pltpu.SemaphoreType.DMA(shape)


def per_device(features, conv_weight, down_weight, cotangent, src_table, send_list, child_map):
    hbm = pl.BlockSpec(memory_space=pl.ANY)
    vmem, smem, i32 = pltpu.VMEM, pltpu.SMEM, jnp.int32
    coarse, grad_input, grad_conv, grad_down = pl.pallas_call(
        block_kernel,
        out_shape=(
            jax.ShapeDtypeStruct((1, 512, 128), BF16),
            jax.ShapeDtypeStruct((4, 8, 8, 512), BF16),
            jax.ShapeDtypeStruct((27, C, C), F32),
            jax.ShapeDtypeStruct((C, 128), F32),
        ),
        in_specs=[hbm] * 6 + [pl.BlockSpec(memory_space=pltpu.SMEM)],
        out_specs=(hbm,) * 4,
        scratch_shapes=[
            vmem((4, 8, 8, 512), BF16), vmem((27, C, C), BF16), vmem((C, 128), BF16), vmem((1, 512, 128), BF16),
            smem((4, 26), i32), vmem((4, 26), i32), vmem((8, 128), i32),
            smem((1, PEERS, 4), i32), vmem((1, PEERS, 4), i32), vmem((16, 128), i32), smem((16, 128), i32),
            vmem((1024, 128), F32),
            vmem((LOCAL, 16, 256), BF16),
            vmem((TABLE, 16, 256), BF16),
            vmem((NEAR, 4, 16, 256), BF16),
            vmem((NEAR, 4, 16, 256), BF16),
            vmem((8, 128), i32), vmem((N_SUB, 8, 128), i32),
            vmem((128, 128), BF16),
            vmem((N_SUB, 32, 128), BF16), vmem((N_SUB, 32, 128), BF16),
            vmem((512, 512), BF16),
            vmem((9, 256, 128), BF16), vmem((9, 128, 256), BF16),
            vmem((256, 128), F32), vmem((1280, 128), F32),
            vmem((3, 320, 640), BF16),
            vmem((1024, 128), F32),
            vmem((384, 768), BF16),
            vmem((128, 1024), BF16),
            vmem((15 * 320, 128), F32),
            vmem((TERMS + 1, 8, 512), F32),
            vmem((1024, 128), F32),
            vmem((32, 128), BF16), vmem((N_SUB, 32, 128), BF16),
            vmem((N_GRP, 128, 128), F32), vmem((N_GRP, 128, 128), F32), vmem((128, 128), F32),
            vmem((N_SUB, 8, 128), F32), vmem((8, 128), F32), vmem((N_SUB, 8, 128), F32),
            vmem((128, 128), BF16), vmem((N_GRP, 128, 128), BF16),
            vmem((SLOTS + 1, 8, 512), F32),
            vmem((1, 512, 128), BF16), vmem((4, 8, 8, 512), BF16), vmem((27, C, C), F32), vmem((C, 128), F32),
        ]
        + [dma(NEAR)] * 4
        + [dma(N_SUB)] * 6
        + [dma(N_GRP)] * 4
        + [dma(N_SUB)] * 4
        + [dma(N_GRP)] * 2
        + [dma(9), dma(4)],
        compiler_params=pltpu.CompilerParams(
            collective_id=0, has_side_effects=True, vmem_limit_bytes=VMEM_LIMIT
        ),
        name="block",
    )(features, conv_weight, down_weight, cotangent, src_table, send_list, child_map)
    return coarse, grad_input, grad_conv, grad_down


def solution(mesh):
    both = ("grp", "sub")
    placed = (
        P(both, None, None, None),
        P(),
        P(),
        P(both, None, None),
        P(both, None),
        P(both, None, None),
        P(both),
    )
    return jax.shard_map(
        per_device,
        mesh=mesh,
        in_specs=placed,
        out_specs=(P(both, None, None), P(both, None, None, None), P(), P()),
        check_vma=False,
    )
```

profile of v0, /device:TPU:1, one launch (start us, length us, event | category | flops | bytes accessed | tf_op | source)
XLA Modules:
  0.0 69.8 jit_solution(6536139133463100731)
XLA Ops:
  0.6 1.4 %copy.11.send_h = s32[1,128,4]{2,1,0:T(8,128)} copy(s32[1,128,4]{1,2,0:T(4,128)} %param.12) | data formatting | bytes 4096 | tf_op args[5]
  2.0 62.6 %block.1 = (bf16[1,512,128]{2,1,0:T(8,128)(2,1)}, bf16[4,8,8,512]{3,2,1,0:T(8,128)(2,1)}, f32[27,64,64]{2,1,0:T(8,128)}, f32[64,128]{1,0:T(8,128)}) custom-call(bf16[4,8,8,512]{3,2,1,0:T(8,128)(2,1)} %feat_h.1, bf16[27,64,64]{2,1,0:T(8,128)(2,1)} %cw_h.1, bf16[64,128]{1,0:T(8,128)(2,1)} %dw_h.1, bf16[1,512,128]{2,1,0:T(8,128)(2,1)} %cot_h.1, s32[4,26]{1,0:T(4,128)} %src_h.1, ...), custom_call_target="tpu_custom_call" | custom-call | tf_op jit(solution)/shard_map/block/pallas_call | solution.py:681
  64.6 0.0 copy-start
  64.7 1.6 %copy.16 = bf16[1,512,128]{2,1,0:T(8,128)(2,1)} copy(bf16[1,512,128]{2,1,0:T(8,128)(2,1)} %get-tuple-element.8) | data formatting | bytes 262144
  66.3 0.0 copy-done
  66.3 0.7 %copy.17 = bf16[4,8,8,512]{3,2,1,0:T(8,128)(2,1)} copy(bf16[4,8,8,512]{3,2,1,0:T(8,128)(2,1)S(1)} %copy-done) | data formatting | bytes 524288
  67.0 0.0 copy-start.1
  67.0 2.2 %copy.18 = f32[27,64,64]{2,1,0:T(8,128)} copy(f32[27,64,64]{2,1,0:T(8,128)} %get-tuple-element.10) | data formatting | bytes 884736
  69.2 0.0 copy-done.1
  69.2 0.6 copy.19
Async XLA Ops:
  64.6 1.6 %copy-start = (bf16[4,8,8,512]{3,2,1,0:T(8,128)(2,1)S(1)}, bf16[4,8,8,512]{3,2,1,0:T(8,128)(2,1)}, u32[]{:S(2)}) copy-start(bf16[4,8,8,512]{3,2,1,0:T(8,128)(2,1)} %get-tuple-element.9) | copy-start | bytes 786436
  67.0 2.2 %copy-start.1 = (f32[64,128]{1,0:T(8,128)S(1)}, f32[64,128]{1,0:T(8,128)}, u32[]{:S(2)}) copy-start(f32[64,128]{1,0:T(8,128)} %get-tuple-element.11) | copy-start | bytes 98308
where the time goes:
time: 70 us; the launch traced here: 69.8 us
  Pallas kernels  62.6 us (89%)
  local copies, waits for them, and re-layouts  6.53 us (9%)
    pallas_call x1, Pallas kernels, per_device(): pl.pallas_call(block_kernel, out_shape=(jax.ShapeDtypeStruct((1, 512, 128...  62.6 us
    unnamed x9, local copies, waits for them, and re-layouts  6.53 us

commit v1 on v0

--- a/solution.py
+++ b/solution.py
@@ -5,7 +5,7 @@
 from jax.experimental.pallas import tpu as pltpu
 from jax.sharding import PartitionSpec as P
 
-MESH = pl.DeviceIdType.MESH
+LOGICAL = pl.DeviceIdType.LOGICAL
 N_GRP, N_SUB = 8, 16
 PEERS = N_GRP * N_SUB
 NEAR = 33
@@ -16,6 +16,7 @@
 TABLE = DUMP + 4
 VMEM_LIMIT = 58 * 1024 * 1024
 TERMS = 4 * 26
+FIRST_FACES = NEAR
 SLOTS = 4 * NEAR
 
 OFFSETS = [
@@ -40,10 +41,6 @@
     return jnp.where(step <= 16, step - 1, jnp.where(step == 64, 16, step - 95))
 
 
-def coords(device):
-    return (device // N_SUB, device % N_SUB)
-
-
 def lane_iota(rows):
     return lax.broadcasted_iota(jnp.int32, (rows, 128), 1)
 
@@ -92,12 +89,12 @@
     grouped = value.reshape(rows // 8, 8, 128)
     return pltpu.roll(grouped, shift % 8, axis=1).reshape(rows, 128)
 
-def loop(count, body, start=0):
+def loop(count, body, start=0, unroll=True):
     def step(i, _):
         body(i)
         return 0
 
-    lax.fori_loop(start, count, step, 0)
+    lax.fori_loop(start, count, step, 0, unroll=unroll)
 
 
 def column_max(value):
@@ -141,8 +138,8 @@
     def number(device):
         return 4 * jnp.clip(near_of((device - me) & (PEERS - 1)), 0, NEAR - 1)
 
-    columns = [jnp.broadcast_to(send_v[:, k : k + 1], whole) for k in range(4)]
-    rows = [column.T for column in columns]
+    rows = [jnp.broadcast_to(send_v[k : k + 1, :], whole) for k in range(4)]
+    columns = [row.T for row in rows]
     first, second = number(below), number(along)
     for k in range(4):
         cases = []
@@ -155,14 +152,12 @@
 
 def block_kernel(
     feat_h, cw_h, dw_h, cot_h, src_h, send_h, child_s,
-    coarse_h, grad_h, conv_h, down_h,
+    coarse_h, grad_h, ag2,
     feat, cw, dw, cot, src_s, src_p, src_v, send_s, send_v, ids, ids_s,
     flat, faces, table, sbuf, returned, key_s, key_r, dwp, tg_s, tg_r, place,
     band, bandt, zrim, yrim, pad, pre, pg, pgt, acc_a, term, inner,
-    tile_s, tile_r, convt, rs1, tot, rs2, fin, ag1, ag1b, ag2, chain,
-    coarse, grad, conv_v, down_v,
-    face_ss, face_rs, back_ss, back_rs, key_ss, key_rs, tg_ss, tg_rs, tile_ss, tile_rs,
-    one_ss, one_rs, oneb_ss, oneb_rs, two_ss, two_rs, three_ss, three_rs, four_ss, four_rs, in_sem, out_sem,
+    tile_s, tile_r, convt, rs1, tot, rs2, fin, ag1, ag1b, chain, coarse, grad,
+    face_sem, back_rs, key_sem, tg_sem, tile_sem, one_sem, two_sem, three_sem, four_sem, in_sem, out_sem,
 ):
     grp, sub = lax.axis_index("grp"), lax.axis_index("sub")
     me = grp * N_SUB + sub
@@ -170,14 +165,14 @@
     barrier = pltpu.get_barrier_semaphore()
 
     def signal(peer):
-        pl.semaphore_signal(barrier, inc=1, device_id=peer, device_id_type=MESH)
+        pl.semaphore_signal(barrier, inc=1, device_id=peer, device_id_type=LOGICAL)
 
     def near_peer(j):
-        return coords(lax.rem(me + step_of(j), PEERS))
+        return (me + step_of(j)) & (PEERS - 1)
 
     loop(NEAR, lambda j: signal(near_peer(j)))
     for far in (2, 3, 5, 6):
-        signal((lax.rem(grp + far, N_GRP), sub))
+        signal(((grp + far) & (N_GRP - 1)) * N_SUB + sub)
 
     loads = [
         pltpu.make_async_copy(source, target, in_sem.at[i])
@@ -223,76 +218,90 @@
     loads[1].wait()
 
     def pack(j):
-        peer = lax.rem(me + step_of(j), PEERS)
+        peer = near_peer(j)
         for k in range(4):
-            sbuf[j, k] = faces[jnp.maximum(send_s[0, peer, k], 0)]
-
-    loop(NEAR, pack)
+            sbuf[j, k] = faces[jnp.maximum(send_s[k, peer], 0)]
+
+    loop(NEAR, pack, unroll=3)
     key_s[4:8] = jnp.zeros((4, 128), jnp.int32)
     key_r[sub] = key_s[...]
     pl.semaphore_wait(barrier, NEAR + 4)
 
-    def sub_copy(s, src, dst, send_sem, recv_sem, arrival):
-        other = lax.rem(sub + s, N_SUB)
-        slot = other if arrival else sub
+    def sub_copy(s, src, dst, sems):
+        other = (sub + s) & (N_SUB - 1)
         return pltpu.make_async_remote_copy(
-            src_ref=src(other), dst_ref=dst.at[slot], send_sem=send_sem.at[other], recv_sem=recv_sem.at[slot],
-            device_id=(grp, other), device_id_type=MESH,
-        )
-
-    def grp_copy(s, src, dst, send_sem, recv_sem, arrival):
-        other = lax.rem(grp + s, N_GRP)
-        slot = other if arrival else grp
+            src_ref=src(other), dst_ref=dst.at[sub], send_sem=sems.at[0], recv_sem=sems.at[1],
+            device_id=grp * N_SUB + other, device_id_type=LOGICAL,
+        )
+
+    def grp_copy(s, src, dst, sems):
+        other = (grp + s) & (N_GRP - 1)
         return pltpu.make_async_remote_copy(
-            src_ref=src(other), dst_ref=dst(slot), send_sem=send_sem.at[other], recv_sem=recv_sem.at[slot],
-            device_id=(other, sub), device_id_type=MESH,
-        )
-
-    def near_copy(j, dst, send_sem, recv_sem, arrival):
-        slot = j if arrival else twin(j)
+            src_ref=src(other), dst_ref=dst(grp), send_sem=sems.at[0], recv_sem=sems.at[1],
+            device_id=other * N_SUB + sub, device_id_type=LOGICAL,
+        )
+
+    def near_copy(j, dst, send_sem, recv_sem):
         return pltpu.make_async_remote_copy(
-            src_ref=sbuf.at[j], dst_ref=dst(slot), send_sem=send_sem.at[j], recv_sem=recv_sem.at[slot],
-            device_id=near_peer(j), device_id_type=MESH,
-        )
-
-    def key_copy(s, arrival):
-        return sub_copy(s, lambda other: key_s, key_r, key_ss, key_rs, arrival)
-
-    def tg_copy(s, arrival):
-        return sub_copy(s, lambda other: tg_s.at[other], tg_r, tg_ss, tg_rs, arrival)
-
-    def tile_copy(s, arrival):
-        return sub_copy(s, lambda other: tile_s, tile_r, tile_ss, tile_rs, arrival)
-
-    def face_copy(j, arrival):
-        return near_copy(j, lambda slot: table.at[pl.ds(LOCAL + 4 * slot, 4)], face_ss, face_rs, arrival)
-
-    def back_copy(j, arrival):
-        return near_copy(j, lambda slot: returned.at[slot], back_ss, back_rs, arrival)
-
-    def one_copy(s, arrival):
+            src_ref=sbuf.at[j], dst_ref=dst, send_sem=send_sem, recv_sem=recv_sem,
+            device_id=near_peer(j), device_id_type=LOGICAL,
+        )
+
+    def all_of(ref, sems):
+        return pltpu.make_async_remote_copy(
+            src_ref=ref, dst_ref=ref, send_sem=sems.at[0], recv_sem=sems.at[1],
+            device_id=(me + 1) & (PEERS - 1), device_id_type=LOGICAL,
+        )
+
+    def key_copy(s):
+        return sub_copy(s, lambda other: key_s, key_r, key_sem)
+
+    def tg_copy(s):
+        return sub_copy(s, lambda other: tg_s.at[other], tg_r, tg_sem)
+
+    def tile_copy(s):
+        return sub_copy(s, lambda other: tile_s, tile_r, tile_sem)
+
+    def face_copy(j):
+        return near_copy(j, table.at[pl.ds(LOCAL + 4 * twin(j), 4)], face_sem.at[0], face_sem.at[1])
+
+    def back_copy(j):
+        return near_copy(j, returned.at[twin(j)], face_sem.at[2], back_rs.at[twin(j)])
+
+    def back_arrival(j):
+        return near_copy(j, returned.at[j], face_sem.at[2], back_rs.at[j])
+
+    def one_copy(s):
         return grp_copy(
-            s, lambda other: convt.at[other, pl.ds(0, 112)], lambda slot: rs1.at[slot, pl.ds(0, 112)],
-            one_ss, one_rs, arrival,
-        )
-
-    def oneb_copy(s, arrival):
+            s, lambda other: convt.at[other, pl.ds(0, 112)], lambda slot: rs1.at[slot, pl.ds(0, 112)], one_sem
+        )
+
+    def oneb_copy(s):
         return grp_copy(
-            s, lambda other: convt.at[other, pl.ds(112, 16)], lambda slot: rs1.at[slot, pl.ds(112, 16)],
-            oneb_ss, oneb_rs, arrival,
-        )
-
-    def two_copy(s, arrival):
-        return sub_copy(s, lambda other: tot.at[pl.ds(8 * other, 8)], rs2, two_ss, two_rs, arrival)
-
-    def three_copy(s, arrival):
-        return sub_copy(s, lambda other: fin, ag1, three_ss, three_rs, arrival)
-
-    def four_copy(s, arrival):
-        return grp_copy(s, lambda other: ag1b, lambda slot: ag2.at[slot], four_ss, four_rs, arrival)
-
-    loop(N_SUB, lambda s: key_copy(s, False).start(), 1)
-    loop(NEAR, lambda j: face_copy(j, False).start())
+            s, lambda other: convt.at[other, pl.ds(112, 16)], lambda slot: rs1.at[slot, pl.ds(112, 16)], one_sem
+        )
+
+    def two_copy(s):
+        return sub_copy(s, lambda other: tot.at[pl.ds(8 * other, 8)], rs2, two_sem)
+
+    def three_copy(s):
+        return sub_copy(s, lambda other: fin, ag1, three_sem)
+
+    def four_copy(s):
+        return grp_copy(s, lambda other: ag1b, lambda slot: ag2.at[slot], four_sem)
+
+    sub_all, grp_all = pl.ds(0, N_SUB - 1), pl.ds(0, N_GRP - 1)
+    key_all = all_of(key_r.at[sub_all], key_sem)
+    tg_all = all_of(tg_r.at[sub_all], tg_sem)
+    tile_all = all_of(tile_r.at[sub_all], tile_sem)
+    face_all = all_of(table.at[pl.ds(LOCAL, SLOTS)], face_sem)
+    one_all = all_of(rs1.at[grp_all], one_sem)
+    two_all = all_of(rs2.at[sub_all], two_sem)
+    three_all = all_of(ag1.at[sub_all], three_sem)
+    four_all = all_of(ag2.at[grp_all], four_sem)
+
+    loop(N_SUB, lambda s: key_copy(s).start(), 1)
+    loop(FIRST_FACES, lambda j: face_copy(j).start())
 
     for load in loads[2:]:
         load.wait()
@@ -306,11 +315,6 @@
             d = 2 - s
             bandt[n, 0:64, 64 * d : 64 * d + 64] = w
             bandt[n, 64:128, 64 * d + 64 : 64 * d + 128] = w
-    src_v[...] = jnp.full((8, 128), -1, jnp.int32)
-    src_v[0:4, 0:26] = src_p[...]
-    index_tables(src_v, send_v.at[0], ids, me)
-    to_scalars = pltpu.make_async_copy(ids, ids_s, in_sem.at[8])
-    to_scalars.start()
     pg[...] = jnp.zeros_like(pg)
     term[TERMS] = jnp.zeros((8, 512), F32)
     chain[SLOTS] = jnp.zeros((8, 512), F32)
@@ -327,7 +331,7 @@
         inside = 4 * (x & 1) + 2 * (y & 1) + (z & 1)
         return (64 * sub + spot) * 8 + inside
 
-    loop(N_SUB, lambda s: key_copy(s, True).wait_recv(), 1)
+    key_all.wait_recv()
     ijk = row_iota(8)
     keys = jnp.concatenate(
         [jnp.broadcast_to(key_r[s, b : b + 1, :], (8, 128)) + ijk for s in range(N_SUB) for b in range(4)], axis=0
@@ -337,13 +341,19 @@
     tiles = jnp.dot(take, coarse_grad, preferred_element_type=F32).astype(BF16)
     tg_s[...] = tiles.reshape(N_SUB, 32, 128)
     tg_r[sub] = tg_s[sub]
-    loop(N_SUB, lambda s: tg_copy(s, False).start(), 1)
+    loop(N_SUB, lambda s: tg_copy(s).start(), 1)
+    loop(NEAR, lambda j: face_copy(j).start(), FIRST_FACES)
     key_row = jnp.concatenate([keys[128 * q : 128 * q + 128].T for q in range(4)], axis=1)[0:1]
     place[...] = jnp.where(
         jnp.broadcast_to(key_row, (512, 512)) == jnp.broadcast_to(voxel_key((512, 1), 0), (512, 512)), 1.0, 0.0
     ).astype(BF16)
+    src_v[...] = jnp.full((8, 128), -1, jnp.int32)
+    src_v[0:4, 0:26] = src_p[...]
+    index_tables(src_v, send_v, ids, me)
+    to_scalars = pltpu.make_async_copy(ids, ids_s, in_sem.at[8])
+    to_scalars.start()
     to_scalars.wait()
-    loop(NEAR, lambda j: face_copy(j, True).wait_recv())
+    face_all.wait_recv()
 
     def slab(b, offset):
         code = src_s[b, NUMBER[offset]]
@@ -407,7 +417,7 @@
             total = product if total is None else total + product
         pre[256 * m : 256 * m + 256] = total
 
-    loop(N_SUB, lambda s: tg_copy(s, True).wait_recv(), 1)
+    tg_all.wait_recv()
     grad_tile = tg_r[0].astype(F32)
     for s in range(1, N_SUB):
         grad_tile += tg_r[s].astype(F32)
@@ -442,7 +452,7 @@
     pooled = pooled.reshape(32, 128) * (1.0 / 64.0)
     tile_s[...] = jnp.where(lows(32), pooled, 0.0).astype(BF16)
     tile_r[sub] = tile_s[...]
-    loop(N_SUB, lambda s: tile_copy(s, False).start(), 1)
+    loop(N_SUB, lambda s: tile_copy(s).start(), 1)
 
     for m in range(4):
         pgt[:, 256 * m : 256 * m + 256] = (
@@ -477,7 +487,7 @@
             keep(at + 1, jnp.where(low64, held, turned))
             keep(at + 2, jnp.where(low64, turned, half(second)))
     keep(13, jnp.where(low64, held, 0.0))
-    loop(N_GRP, lambda s: one_copy(s, False).start(), 1)
+    loop(N_GRP, lambda s: one_copy(s).start(), 1)
 
     for sy in range(3):
         for m in range(5):
@@ -548,61 +558,61 @@
                 value = term[earlier, :, 128 * q : 128 * q + 128]
                 term[26 * b + t, :, 128 * q : 128 * q + 128] = value if tile is None else value + tile
 
+    face_all.wait_send()
+
     def leave(j):
-        face_copy(j, False).wait_send()
         for k in range(4):
             value = term[ids_s[4 + k, j]]
             sbuf[j, k] = to_face([value[:, 128 * q : 128 * q + 128] for q in range(4)]).astype(BF16)
-        back_copy(j, False).start()
-
-    loop(NEAR, leave)
-
-    loop(N_SUB, lambda s: tile_copy(s, True).wait_recv(), 1)
+        back_copy(j).start()
+
+    loop(11, leave)
+
+    tile_all.wait_recv()
     coarse_in = jnp.dot(place[...], tile_r[...].reshape(512, 128), preferred_element_type=F32)
     dwp[64:128] = jnp.zeros((64, 128), BF16)
     down = jnp.dot(coarse_in.T.astype(BF16), cot[0], preferred_element_type=F32)
     for g in range(N_GRP):
         convt[g, 112:120] = down[8 * g : 8 * g + 8]
         convt[g, 120:128] = jnp.zeros((8, 128), F32)
-    loop(N_GRP, lambda s: oneb_copy(s, False).start(), 1)
+    loop(N_GRP, lambda s: oneb_copy(s).start(), 1)
     coarse[0] = jnp.dot(coarse_in.astype(BF16), dwp[...], preferred_element_type=F32).astype(BF16)
     coarse_store = pltpu.make_async_copy(coarse, coarse_h, out_sem.at[0])
     coarse_store.start()
     rs1[grp] = convt[grp]
 
-    def both_arrivals(s):
-        one_copy(s, True).wait_recv()
-        oneb_copy(s, True).wait_recv()
-
-    loop(N_GRP, both_arrivals, 1)
+    one_all.wait_recv()
     total = rs1[0]
     for g in range(1, N_GRP):
         total += rs1[g]
     tot[...] = total
-    loop(N_SUB, lambda s: two_copy(s, False).start(), 1)
+    loop(N_SUB, lambda s: two_copy(s).start(), 1)
+    loop(22, leave, 11)
     rs2[sub] = tot[pl.ds(pl.multiple_of(8 * sub, 8), 8), :]
-    loop(N_SUB, lambda s: two_copy(s, True).wait_recv(), 1)
+    two_all.wait_recv()
     total = rs2[0]
     for s in range(1, N_SUB):
         total += rs2[s]
     fin[...] = total
-    loop(N_SUB, lambda s: three_copy(s, False).start(), 1)
+    loop(N_SUB, lambda s: three_copy(s).start(), 1)
+    loop(NEAR, leave, 22)
     ag1[sub] = fin[...]
-    loop(N_SUB, lambda s: three_copy(s, True).wait_recv(), 1)
+    three_all.wait_recv()
     ag1b[...] = ag1[...].reshape(128, 128).astype(BF16)
-    loop(N_GRP, lambda s: four_copy(s, False).start(), 1)
-    ag2[grp] = ag1b[...]
+    loop(N_GRP, lambda s: four_copy(s).start(), 1)
+    own_sums = pltpu.make_async_copy(ag1b, ag2.at[grp], out_sem.at[2])
+    own_sums.start()
 
     def take_back(j):
-        back_copy(j, True).wait_recv()
-        peer = lax.rem(me + step_of(j), PEERS)
+        back_arrival(j).wait_recv()
+        peer = near_peer(j)
         for k in range(4):
             value = chain[ids_s[9 + k, peer]]
             tiles = from_face(returned[j, k])
             for q in range(4):
                 chain[4 * j + k, :, 128 * q : 128 * q + 128] = value[:, 128 * q : 128 * q + 128] + tiles[q]
 
-    loop(NEAR, take_back)
+    loop(NEAR, take_back, unroll=3)
 
     face_sums = [term[ids_s[8, f]] + chain[ids_s[13, f]] for f in range(LOCAL)]
 
@@ -640,34 +650,56 @@
     grad_store = pltpu.make_async_copy(grad, grad_h, out_sem.at[1])
     grad_store.start()
 
-    loop(N_GRP, lambda s: four_copy(s, True).wait_recv(), 1)
+    own_sums.wait()
+    four_all.wait_recv()
+
+    for group in (key_all, tg_all, tile_all, one_all, two_all, three_all, four_all):
+        group.wait_send()
+    pltpu.make_async_remote_copy(
+        src_ref=sbuf, dst_ref=returned, send_sem=face_sem.at[2], recv_sem=face_sem.at[1],
+        device_id=(me + 1) & (PEERS - 1), device_id_type=LOGICAL,
+    ).wait_send()
+    for store in (coarse_store, grad_store):
+        store.wait()
+
+
+def finish_kernel(
+    coarse, grad, sums, coarse_o, grad_o, conv_o, down_o, coarse_v, grad_v, ag2, conv_v, down_v, loaded, sems
+):
+    loads = [
+        pltpu.make_async_copy(source, target, loaded.at[i])
+        for i, (source, target) in enumerate(((sums, ag2), (coarse, coarse_v), (grad, grad_v)))
+    ]
+    for load in loads:
+        load.start()
+    for load in loads:
+        load.wait()
+    stores = [
+        pltpu.make_async_copy(coarse_v, coarse_o, sems.at[0]), pltpu.make_async_copy(grad_v, grad_o, sems.at[1])
+    ]
+    for store in stores:
+        store.start()
     got = [ag2[g].astype(F32) for g in range(N_GRP)]
+
+    def save(source, target, number):
+        stores.append(pltpu.make_async_copy(source, target, sems.at[number]))
+        stores[-1].start()
+
     for s in range(15):
         value = jnp.concatenate([got[g][8 * s : 8 * s + 8] for g in range(N_GRP)], axis=0)
         if s == 14:
             down_v[...] = value
-        else:
-            turned = value.T
-            conv_v[2 * s] = turned[0:64]
-            if s < 13:
-                conv_v[2 * s + 1] = turned[64:128]
-    conv_store = pltpu.make_async_copy(conv_v, conv_h, out_sem.at[2])
-    conv_store.start()
-    down_store = pltpu.make_async_copy(down_v, down_h, out_sem.at[3])
-    down_store.start()
-
-    def sub_ends(s):
-        for copy in (key_copy, tg_copy, tile_copy, two_copy, three_copy):
-            copy(s, False).wait_send()
-
-    def grp_ends(s):
-        for copy in (one_copy, oneb_copy, four_copy):
-            copy(s, False).wait_send()
-
-    loop(N_SUB, sub_ends, 1)
-    loop(N_GRP, grp_ends, 1)
-    loop(NEAR, lambda j: back_copy(j, False).wait_send())
-    for store in (coarse_store, grad_store, conv_store, down_store):
+            save(down_v, down_o, 6)
+            continue
+        turned = value.T
+        conv_v[2 * s] = turned[0:64]
+        if s < 13:
+            conv_v[2 * s + 1] = turned[64:128]
+        if s in (3, 6, 9, 13):
+            first, last = {3: (0, 8), 6: (8, 14), 9: (14, 20), 13: (20, 27)}[s]
+            part = pl.ds(first, last - first)
+            save(conv_v.at[part], conv_o.at[part], {3: 2, 6: 3, 9: 4, 13: 5}[s])
+    for store in stores:
         store.wait()
 
 
@@ -678,20 +710,19 @@
 def per_device(features, conv_weight, down_weight, cotangent, src_table, send_list, child_map):
     hbm = pl.BlockSpec(memory_space=pl.ANY)
     vmem, smem, i32 = pltpu.VMEM, pltpu.SMEM, jnp.int32
-    coarse, grad_input, grad_conv, grad_down = pl.pallas_call(
+    coarse, grad_input, sums = pl.pallas_call(
         block_kernel,
         out_shape=(
             jax.ShapeDtypeStruct((1, 512, 128), BF16),
             jax.ShapeDtypeStruct((4, 8, 8, 512), BF16),
-            jax.ShapeDtypeStruct((27, C, C), F32),
-            jax.ShapeDtypeStruct((C, 128), F32),
+            jax.ShapeDtypeStruct((N_GRP, 128, 128), BF16),
         ),
         in_specs=[hbm] * 6 + [pl.BlockSpec(memory_space=pltpu.SMEM)],
-        out_specs=(hbm,) * 4,
+        out_specs=(hbm,) * 3,
         scratch_shapes=[
             vmem((4, 8, 8, 512), BF16), vmem((27, C, C), BF16), vmem((C, 128), BF16), vmem((1, 512, 128), BF16),
             smem((4, 26), i32), vmem((4, 26), i32), vmem((8, 128), i32),
-            smem((1, PEERS, 4), i32), vmem((1, PEERS, 4), i32), vmem((16, 128), i32), smem((16, 128), i32),
+            smem((4, PEERS), i32), vmem((4, PEERS), i32), vmem((16, 128), i32), smem((16, 128), i32),
             vmem((1024, 128), F32),
             vmem((LOCAL, 16, 256), BF16),
             vmem((TABLE, 16, 256), BF16),
@@ -713,22 +744,35 @@
             vmem((32, 128), BF16), vmem((N_SUB, 32, 128), BF16),
             vmem((N_GRP, 128, 128), F32), vmem((N_GRP, 128, 128), F32), vmem((128, 128), F32),
             vmem((N_SUB, 8, 128), F32), vmem((8, 128), F32), vmem((N_SUB, 8, 128), F32),
-            vmem((128, 128), BF16), vmem((N_GRP, 128, 128), BF16),
+            vmem((128, 128), BF16),
             vmem((SLOTS + 1, 8, 512), F32),
-            vmem((1, 512, 128), BF16), vmem((4, 8, 8, 512), BF16), vmem((27, C, C), F32), vmem((C, 128), F32),
+            vmem((1, 512, 128), BF16), vmem((4, 8, 8, 512), BF16),
         ]
-        + [dma(NEAR)] * 4
-        + [dma(N_SUB)] * 6
-        + [dma(N_GRP)] * 4
-        + [dma(N_SUB)] * 4
-        + [dma(N_GRP)] * 2
-        + [dma(9), dma(4)],
+        + [dma(3), dma(NEAR)]
+        + [dma(2)] * 7
+        + [dma(9), dma(3)],
         compiler_params=pltpu.CompilerParams(
             collective_id=0, has_side_effects=True, vmem_limit_bytes=VMEM_LIMIT
         ),
         name="block",
-    )(features, conv_weight, down_weight, cotangent, src_table, send_list, child_map)
-    return coarse, grad_input, grad_conv, grad_down
+    )(features, conv_weight, down_weight, cotangent, src_table, send_list[0].T, child_map)
+    return pl.pallas_call(
+        finish_kernel,
+        out_shape=(
+            jax.ShapeDtypeStruct((1, 512, 128), BF16),
+            jax.ShapeDtypeStruct((4, 8, 8, 512), BF16),
+            jax.ShapeDtypeStruct((27, C, C), F32),
+            jax.ShapeDtypeStruct((C, 128), F32),
+        ),
+        in_specs=[hbm] * 3,
+        out_specs=(hbm,) * 4,
+        scratch_shapes=[
+            vmem((1, 512, 128), BF16), vmem((4, 8, 8, 512), BF16),
+            vmem((N_GRP, 128, 128), BF16), vmem((27, C, C), F32), vmem((C, 128), F32), dma(3), dma(7),
+        ],
+        compiler_params=pltpu.CompilerParams(vmem_limit_bytes=VMEM_LIMIT),
+        name="finish",
+    )(coarse, grad_input, sums)
 
 
 def solution(mesh):

time: 70 us -> 57.8 us (0.83); the launches traced: 69.8 us -> 56.8 us
  local copies, waits for them, and re-layouts: 6.53 us -> 0 us
  Pallas kernels: 62.6 us -> 56.1 us
    pallas_call x1, Pallas kernels: 62.6 us -> 53.9 us  [per_device(): pl.pallas_call(block_kernel, out_shape=(jax.ShapeDtypeStruct((1, 512, 128...]
    unnamed x9 -> x0, local copies, waits for them, and re-layouts: 6.53 us -> none
    pallas_call x0 -> x1, Pallas kernels: none -> 2.21 us  [per_device(): pl.pallas_call(finish_kernel, out_shape=(jax.ShapeDtypeStruct((1, 512, 12...]
where the time goes in v1:
time: 57.8 us; the launch traced here: 56.8 us
  Pallas kernels  56.1 us (97%)
  between operations  0.64 us (1%)
    pallas_call x1, Pallas kernels, per_device(): pl.pallas_call(block_kernel, out_shape=(jax.ShapeDtypeStruct((1, 512, 128...  53.9 us
    pallas_call x1, Pallas kernels, per_device(): pl.pallas_call(finish_kernel, out_shape=(jax.ShapeDtypeStruct((1, 512, 12...  2.21 us

profile of v1, /device:TPU:1, one launch (start us, length us, event | category | flops | bytes accessed | tf_op | source)
XLA Modules:
  0.0 56.8 jit_solution(7853103341365427508)
XLA Ops:
  0.6 53.9 %block.1 = (bf16[1,512,128]{2,1,0:T(8,128)(2,1)}, bf16[4,8,8,512]{3,2,1,0:T(8,128)(2,1)}, bf16[8,128,128]{2,1,0:T(8,128)(2,1)}) custom-call(bf16[4,8,8,512]{3,2,1,0:T(8,128)(2,1)} %feat_h.1, bf16[27,64,64]{2,1,0:T(8,128)(2,1)} %cw_h.1, bf16[64,128]{1,0:T(8,128)(2,1)} %dw_h.1, bf16[1,512,128]{2,1,0:T(8,128)(2,1)} %cot_h.1, s32[4,26]{1,0:T(4,128)} %src_h.1, ...), custom_call_target="tpu_custom_call" | custom-call | tf_op jit(solution)/shard_map/block/pallas_call | solution.py:713
  54.5 2.2 %finish.1 = (bf16[1,512,128]{2,1,0:T(8,128)(2,1)}, bf16[4,8,8,512]{3,2,1,0:T(8,128)(2,1)}, f32[27,64,64]{2,1,0:T(8,128)}, f32[64,128]{1,0:T(8,128)}) custom-call(bf16[1,512,128]{2,1,0:T(8,128)(2,1)} %get-tuple-element.7.coarse, bf16[4,8,8,512]{3,2,1,0:T(8,128)(2,1)} %get-tuple-element.8.grad, bf16[8,128,128]{2,1,0:T(8,128)(2,1)} %get-tuple-element.9.sums), custom_call_target="tpu_custom_call" | custom-call | tf_op jit(solution)/shard_map/finish/pallas_call | solution.py:759
